TPU v7x, 512 devices: a whole 4x8x8 slice. The times are simulated.
512 devices in a mesh: tok: 8 (over x, core), exp: 64 (over y, z).
Axes of the slice: x: 4, y: 8, z: 8, core: 2. Of those that a mesh axis runs over, the one named last changes fastest.
Arguments:
- tokens: bfloat16 [4096, 16384], P('exp', 'tok'), as said below
- w_router: bfloat16 [4096, 256], P('exp'), as said below
- pick_lists: int32 [8, 64, 16], P('tok'), may hold values from 0 to 2047, as said below
- w_gate: bfloat16 [64, 4096, 1024], P('exp', None, 'tok'), may hold values from -0.09375 to 0.09375
- w_up: bfloat16 [64, 4096, 1024], P('exp', None, 'tok'), may hold values from -0.09375 to 0.09375
- w_down: bfloat16 [64, 1024, 4096], P('exp', 'tok'), may hold values from -0.1875 to 0.1875
- out_grad: bfloat16 [4096, 16384], P('exp', 'tok'), may hold values from -6 to 6
Outputs:
- layer_out: bfloat16 [4096, 16384], P('exp', 'tok')
- token_grad: bfloat16 [4096, 16384], P('exp', 'tok')
- grad_router: float32 [4096, 256], P('exp')
Inputs may be any that keep to these rules, and one draw needn't show every extreme that they name: `pick_lists`: each of the 64 lists of a group names 16 distinct positions among the group's 2048 tokens. `tokens`: activations. `w_router`: router weights.
All inputs are finite; a program needn't handle non-finite values.
Results may differ from a plain program's by a relative error of at most 0.024.
Values may be sent and summed in bfloat16 or wider, within the bound.
A program may use at most 64 MiB of HBM per device.

v0:
```python
import jax
import jax.numpy as jnp
from jax import lax
from jax.sharding import PartitionSpec as P


def body(tokens, w_router, pick_lists, w_gate, w_up, w_down, out_grad):
    exp_count = lax.axis_size("exp")
    feat_local, group_size = tokens.shape
    local_lists = pick_lists[0]
    capacity = local_lists.shape[1]
    own_index = lax.axis_index("exp")
    own_list = lax.dynamic_index_in_dim(local_lists, own_index, 0, keepdims=False)
    flat_list = local_lists.reshape(-1)
    gate_local = w_gate[0]
    up_local = w_up[0]
    down_local = w_down[0]
    hidden_width = gate_local.shape[1]
    contract_first = (((0,), (0,)), ((), ()))
    contract_last = (((1,), (1,)), ((), ()))

    def select_rows(field):
        picked = field[:, flat_list].reshape(feat_local, exp_count, capacity)
        return jnp.transpose(picked, (1, 0, 2)).reshape(exp_count, feat_local * capacity)

    def assemble(arrived):
        return arrived.reshape(exp_count * feat_local, capacity)

    def spread(feature_rows):
        return feature_rows.reshape(exp_count, feat_local * capacity)

    def collect(arrived):
        shaped = arrived.reshape(exp_count, feat_local, capacity)
        return (
            jnp.transpose(shaped, (1, 0, 2))
            .reshape(feat_local, exp_count * capacity)
            .astype(jnp.float32)
        )

    sent_tokens = select_rows(tokens)
    sent_grads = select_rows(out_grad)
    arrived_tokens = lax.all_to_all(sent_tokens, "exp", split_axis=0, concat_axis=0, tiled=True)
    token_cols = assemble(arrived_tokens)
    local_logits = lax.psum_scatter(
        lax.dot_general(w_router, tokens, contract_first, preferred_element_type=jnp.float32),
        "exp",
        scatter_dimension=0,
        tiled=True,
    )
    peak_score = lax.pmax(jnp.max(local_logits, axis=0), "exp")
    exp_sum = lax.psum(jnp.sum(jnp.exp(local_logits - peak_score), axis=0), "exp")
    router_probs = jnp.exp(local_logits - peak_score) / exp_sum
    own_probs = router_probs[0]
    pick_weight = own_probs[own_list]
    shard_piece = lax.all_gather(token_cols, "tok", axis=1, tiled=True)
    gate_part = lax.dot_general(
        shard_piece, gate_local, contract_first, preferred_element_type=jnp.float32
    )
    up_part = lax.dot_general(
        shard_piece, up_local, contract_first, preferred_element_type=jnp.float32
    )
    pre_joint = jnp.concatenate((gate_part, up_part), axis=1)
    pre_gate = pre_joint[:, :hidden_width]
    pre_up = pre_joint[:, hidden_width:]
    hidden = (jax.nn.silu(pre_gate) * pre_up).astype(jnp.bfloat16)
    row_part = hidden
    expert_out = lax.psum_scatter(
        jnp.dot(row_part, down_local, preferred_element_type=jnp.float32).astype(jnp.bfloat16),
        "tok",
        scatter_dimension=0,
        tiled=True,
    ).astype(jnp.float32)
    weighted = (pick_weight[:, None] * expert_out).astype(jnp.bfloat16)
    returned = lax.all_to_all(spread(weighted.T), "exp", split_axis=0, concat_axis=0, tiled=True)
    layer_out = (
        jnp.zeros((feat_local, group_size), jnp.float32).at[:, flat_list].add(collect(returned))
    )
    arrived_grads = lax.all_to_all(sent_grads, "exp", split_axis=0, concat_axis=0, tiled=True)
    grad_float = assemble(arrived_grads).astype(jnp.float32)
    gate_grad = jnp.sum(grad_float * expert_out.T, axis=0)
    row_grad = (grad_float * pick_weight[None, :]).astype(jnp.bfloat16)
    hidden_grad = lax.dot_general(
        lax.all_gather(row_grad, "tok", axis=1, tiled=True),
        down_local,
        (((0,), (1,)), ((), ())),
        preferred_element_type=jnp.float32,
    )
    sigmoid_gate = jax.nn.sigmoid(pre_gate)
    grad_gate_pre = (
        hidden_grad * pre_up * sigmoid_gate * (1.0 + pre_gate * (1.0 - sigmoid_gate))
    ).astype(jnp.bfloat16)
    grad_up_pre = (hidden_grad * pre_gate * sigmoid_gate).astype(jnp.bfloat16)
    pre_grads = jnp.concatenate((grad_gate_pre, grad_up_pre), axis=1)
    row_part = pre_grads
    gate_term = lax.dot_general(
        row_part[:, :hidden_width], gate_local, contract_last, preferred_element_type=jnp.float32
    )
    up_term = lax.dot_general(
        row_part[:, hidden_width:], up_local, contract_last, preferred_element_type=jnp.float32
    )
    row_input = lax.psum_scatter(
        (gate_term + up_term).astype(jnp.bfloat16), "tok", scatter_dimension=0, tiled=True
    )
    back_rows = lax.all_to_all(spread(row_input.T), "exp", split_axis=0, concat_axis=0, tiled=True)
    router_float = w_router.astype(jnp.float32)
    token_float = tokens.astype(jnp.float32)
    own_score_grad = jnp.zeros((group_size,), jnp.float32).at[own_list].add(gate_grad)
    pick_sum = lax.psum(router_probs[0] * own_score_grad, "exp")
    local_score_grad = jnp.zeros_like(router_probs).at[0].set(own_score_grad)
    logit_grad = router_probs * (local_score_grad - pick_sum)
    shard_piece = lax.all_gather(logit_grad, "exp", axis=0, tiled=True)
    input_sum = jnp.dot(router_float, shard_piece, precision=lax.Precision.HIGHEST)
    weight_grad = lax.dot_general(
        token_float, shard_piece, contract_last, precision=lax.Precision.HIGHEST
    )
    row_part_grad = (
        jnp.zeros((feat_local, group_size), jnp.float32).at[:, flat_list].add(collect(back_rows))
    )
    token_grad = (input_sum + row_part_grad).astype(jnp.bfloat16)
    grad_router = lax.psum(weight_grad, "tok")
    return (layer_out.astype(jnp.bfloat16), token_grad, grad_router)


def solution(mesh):
    placed = (
        P("exp", "tok"),
        P("exp", None),
        P("tok", None, None),
        P("exp", None, "tok"),
        P("exp", None, "tok"),
        P("exp", "tok", None),
        P("exp", "tok"),
    )
    return jax.shard_map(
        body,
        mesh=mesh,
        in_specs=placed,
        out_specs=(P("exp", "tok"), P("exp", "tok"), P("exp", None)),
        check_vma=False,
    )
```

profile of v0, /device:TPU:1, one launch (start us, length us, event | category | flops | bytes accessed | tf_op | source)
XLA Modules:
  0.0 826.2 jit_solution(15431874208018116715)
XLA Ops:
  10.3 3.2 gather_fusion.1
  15.4 28.4 %all_to_all.38 = bf16[64,2,512]{2,1,0:T(2,128)(2,1)S(1)} all-to-all(bf16[64,2,512]{2,1,0:T(2,128)(2,1)S(1)} %reshape.208), channel_id=1, replica_groups=mesh['tok'=8,'exp'=64] {'exp'}, dimensions={0} | all-to-all | bytes 262144 | tf_op jit(solution)/shard_map/all_to_all | solution.py:42
  46.6 1.7 fusion.28
  48.4 20.5 %all-gather.5.cloned.1.call-done = bf16[4096,128]{0,1:T(8,128)(2,1)} async-done(((bf16[4096,16]{0,1:T(8,128)(2,1)}), bf16[4096,128]{0,1:T(8,128)(2,1)}) %all-gather.5.cloned.1.call-update) | async-done | bytes 1048592 | tf_op jit(solution)/shard_map/all_gather | solution.py:55
  68.9 1.8 fusion.9
  72.9 3.2 gather_fusion.2
  78.1 12.8 %all-to-all-start.2 = ((bf16[64,2,512]{2,1,0:T(2,128)(2,1)}), bf16[64,2,512]{2,1,0:T(2,128)(2,1)S(1)}, u32[]{:S(2)}, u32[]{:S(2)}) async-start(bf16[64,2,512]{2,1,0:T(2,128)(2,1)} %reshape.212), calls=%async_computation.3 | async-start | bytes 262144 | tf_op jit(solution)/shard_map/all_to_all | solution.py:78
  93.1 9.3 %all-to-all-done.2 = bf16[64,2,512]{2,1,0:T(2,128)(2,1)S(1)} async-done(((bf16[64,2,512]{2,1,0:T(2,128)(2,1)}), bf16[64,2,512]{2,1,0:T(2,128)(2,1)S(1)}, u32[]{:S(2)}, u32[]{:S(2)}) %all-to-all-start.2) | async-done | bytes 131104 | tf_op jit(solution)/shard_map/all_to_all | solution.py:78
  106.9 95.4 %all-reduce.7.cloned.1.call-done = f32[256,2048]{1,0:T(8,128)} async-done(((f32[256,2048]{1,0:T(8,128)}), f32[256,2048]{1,0:T(8,128)}) %all-reduce.7.cloned.1.call-update) | async-done | bytes 2097168
  203.2 115.2 %pmax.7 = f32[2048]{0:T(1024)S(1)} all-reduce(f32[2048]{0:T(1024)S(1)} %dynamic-slice_reduce_fusion), channel_id=1, replica_groups=mesh['tok'=8,'exp'=64] {'exp'}, use_global_device_ids=true, to_apply=%region_2.3 | all-reduce | flops 2048 | bytes 16384 | tf_op jit(solution)/shard_map/pmax | solution.py:50
  319.3 112.4 %psum.21 = f32[2048]{0:T(1024)S(1)} all-reduce(f32[2048]{0:T(1024)S(1)} %fusion.21), channel_id=1, replica_groups=mesh['tok'=8,'exp'=64] {'exp'}, use_global_device_ids=true, to_apply=%region_4.5 | all-reduce | flops 2048 | bytes 16384 | tf_op jit(solution)/shard_map/psum | solution.py:51
  433.3 1.8 multiply_convert_fusion
  435.2 84.7 %all-gather.7.cloned.1.call-done = bf16[4096,128]{0,1:T(8,128)(2,1)} async-done(((bf16[4096,16]{0,1:T(8,128)(2,1)}), bf16[4096,128]{0,1:T(8,128)(2,1)}) %all-gather.7.cloned.1.call-update) | async-done | bytes 1048592 | tf_op jit(solution)/shard_map/all_gather | solution.py:83
  519.9 1.7 fusion.1
  525.0 118.6 %psum.22 = f32[2048]{0:T(1024)S(1)} all-reduce(f32[2048]{0:T(1024)S(1)} %mul.55), channel_id=1, replica_groups=mesh['tok'=8,'exp'=64] {'exp'}, use_global_device_ids=true, to_apply=%region_9.10 | all-reduce | flops 2048 | bytes 16384 | tf_op jit(solution)/shard_map/psum | solution.py:108
  647.8 16.5 %all_to_all.39 = bf16[64,2,512]{2,1,0:T(2,128)(2,1)S(1)} all-to-all(bf16[64,2,512]{2,1,0:T(2,128)(2,1)S(1)} %reshape.210), channel_id=1, replica_groups=mesh['tok'=8,'exp'=64] {'exp'}, dimensions={0} | all-to-all | bytes 262144 | tf_op jit(solution)/shard_map/all_to_all | solution.py:74
  665.0 6.3 scatter_custom_fusion
  676.4 4.6 all-to-all-start.3
  681.1 63.3 %all-gather.9.cloned.1.call-done = f32[64,4,2048]{2,1,0:T(4,128)} async-done(((f32[1,4,2048]{2,1,0:T(4,128)}), f32[64,4,2048]{2,1,0:T(4,128)}) %all-gather.9.cloned.1.call-update) | async-done | bytes 2097168 | tf_op jit(solution)/shard_map/all_gather | solution.py:111
  744.4 2.0 reshape.199
  746.4 1.8 convolution_bitcast_fusion.1
  748.3 2.5 convolution_bitcast_fusion
  752.9 6.4 scatter_fusion
  760.3 57.3 %all-reduce.5.cloned.1.call-done = f32[64,256]{1,0:T(8,128)} async-done(((f32[64,256]{1,0:T(8,128)}), f32[64,256]{1,0:T(8,128)}) %all-reduce.5.cloned.1.call-update) | async-done | bytes 65552 | tf_op jit(solution)/shard_map/psum | solution.py:120
  (101 shorter events, 38.3 us)
Async XLA Ops:
  8.0 63.1 %copy-start = (bf16[1,128,4096]{2,1,0:T(8,128)(2,1)S(1)}, bf16[1,128,4096]{2,1,0:T(8,128)(2,1)}, u32[]{:S(2)}) copy-start(bf16[1,128,4096]{2,1,0:T(8,128)(2,1)} %param.14) | copy-start | bytes 3145732
  8.0 60.9 %all-gather.5.cloned.1.call-start = ((), (), s32[]{:S(2)}) async-start(), calls=%async_computation.6 | async-start | bytes 1179648 | tf_op jit(solution)/shard_map/all_gather | solution.py:55
  15.1 31.4 %copy-start.6 = (bf16[64,2048]{1,0:T(8,128)(2,1)S(1)}, bf16[64,2048]{1,0:T(8,128)(2,1)}, u32[]{:S(2)}) copy-start(bf16[64,2048]{1,0:T(8,128)(2,1)} %param.9) | copy-start | bytes 786436
  15.1 31.4 %copy-start.9 = (bf16[64,256]{1,0:T(8,128)(2,1)S(1)}, bf16[64,256]{1,0:T(8,128)(2,1)}, u32[]{:S(2)}) copy-start(bf16[64,256]{1,0:T(8,128)(2,1)} %param.10) | copy-start | bytes 98308
  46.5 22.4 %copy-start.1 = (bf16[1,4096,128]{2,1,0:T(8,128)(2,1)S(1)}, bf16[1,4096,128]{2,1,0:T(8,128)(2,1)}, u32[]{:S(2)}) copy-start(bf16[1,4096,128]{2,1,0:T(8,128)(2,1)} %param.12) | copy-start | bytes 3145732
  46.5 155.8 %all-reduce.7.cloned.1.call-start = ((), (), s32[]{:S(2)}) async-start(), calls=%async_computation.12 | async-start | bytes 4194304
  48.3 22.3 %copy-start.4 = (bf16[1,4096,128]{2,1,0:T(8,128)(2,1)S(1)}, bf16[1,4096,128]{2,1,0:T(8,128)(2,1)}, u32[]{:S(2)}) copy-start(bf16[1,4096,128]{2,1,0:T(8,128)(2,1)} %param.13) | copy-start | bytes 3145732
  48.4 384.9 %reduce-scatter.3.cloned.1.call-start = ((), (), s32[]{:S(2)}) async-start(), calls=%async_computation.7 | async-start | bytes 1179648 | tf_op jit(solution)/shard_map/reduce_scatter | solution.py:67
  68.9 1.8 copy-start.3
  71.1 1.4 copy-start.8
  72.6 20.3 %copy-start.10 = (s32[1,64,16]{1,2,0:T(8,128)S(1)}, s32[1,64,16]{1,2,0:T(8,128)}, u32[]{:S(2)}) copy-start(s32[1,64,16]{1,2,0:T(8,128)} %param.11) | copy-start | bytes 12292
  78.1 24.3 %all-to-all-start.2 = ((bf16[64,2,512]{2,1,0:T(2,128)(2,1)}), bf16[64,2,512]{2,1,0:T(2,128)(2,1)S(1)}, u32[]{:S(2)}, u32[]{:S(2)}) async-start(bf16[64,2,512]{2,1,0:T(2,128)(2,1)} %reshape.212), calls=%async_computation.3 | async-start | bytes 262144 | tf_op jit(solution)/shard_map/all_to_all | solution.py:78
  90.9 429.0 %all-gather.7.cloned.1.call-start = ((), (), s32[]{:S(2)}) async-start(), calls=%async_computation.8 | async-start | bytes 1179648 | tf_op jit(solution)/shard_map/all_gather | solution.py:83
  106.9 414.7 %copy-start.2 = (bf16[1,4096,128]{2,1,0:T(8,128)(2,1)S(1)}, bf16[1,4096,128]{2,1,0:T(8,128)(2,1)}, u32[]{:S(2)}) copy-start(bf16[1,4096,128]{2,1,0:T(8,128)(2,1)} %param.12) | copy-start | bytes 3145732
  435.1 237.1 %reduce-scatter.5.cloned.1.call-start = ((), (), s32[]{:S(2)}) async-start(), calls=%async_computation.9 | async-start | bytes 1179648 | tf_op jit(solution)/shard_map/reduce_scatter | solution.py:101
  521.6 1.2 copy-start.5
  522.8 122.3 %copy-start.7 = (bf16[16,4096]{1,0:T(8,128)(2,1)S(1)}, bf16[16,4096]{1,0:T(8,128)(2,1)}, u32[]{:S(2)}) copy-start(bf16[16,4096]{1,0:T(8,128)(2,1)} %reduce-scatter.3.cloned.1.call-done) | copy-start | bytes 393220
  524.3 220.2 %all-gather.9.cloned.1.call-start = ((), (), s32[]{:S(2)}) async-start(), calls=%async_computation.11 | async-start | bytes 2129920 | tf_op jit(solution)/shard_map/all_gather | solution.py:111
  676.4 75.7 %all-to-all-start.3 = ((bf16[64,2,512]{2,1,0:T(2,128)(2,1)}), bf16[64,2,512]{2,1,0:T(2,128)(2,1)S(1)}, u32[]{:S(2)}, u32[]{:S(2)}) async-start(bf16[64,2,512]{2,1,0:T(2,128)(2,1)} %reshape.214), calls=%async_computation.5 | async-start | bytes 262144 | tf_op jit(solution)/shard_map/all_to_all | solution.py:104
  681.1 136.5 %all-reduce.5.cloned.1.call-start = ((), (), s32[]{:S(2)}) async-start(), calls=%async_computation.10 | async-start | bytes 131072 | tf_op jit(solution)/shard_map/psum | solution.py:120
Sparse Core Ops, SparseCore 0:
  46.6 22.2 all-gather.4
  72.7 35.3 reduce-scatter.2
  435.3 84.5 all-gather.6
  524.4 34.9 reduce-scatter.4
  748.4 69.1 all-reduce.4
Sparse Core Ops, SparseCore 1:
  50.2 152.1 all-reduce.6
  645.2 99.2 all-gather.8
where the time goes:
time: 828 us; the launch traced here: 826 us
  blocking collectives  391 us (47%)
  waiting for transfers between devices  331 us (40%)
  local copies, waits for them, and re-layouts  31.2 us (4%)
  other arithmetic  25.9 us (3%)
  starting transfers between devices  17.7 us (2%)
  between operations  16.4 us (2%)
  matrix products  13.2 us (2%)
    psum x1, blocking collectives, body(): pick_sum = lax.psum(router_probs[0] * own_score_grad, 'exp')  119 us
    pmax x1, blocking collectives, body(): peak_score = lax.pmax(jnp.max(local_logits, axis=0), 'exp')  115 us
    psum x1, blocking collectives, body(): lax.psum(jnp.sum(jnp.exp(local_logits - peak_score), axis=0), 'exp')  112 us
    unnamed x8, waiting for transfers between devices  95.6 us
    all_gather x1, waiting for transfers between devices, body(): lax.all_gather(row_grad, 'tok', axis=1, tiled=True)  84.7 us
    all_gather x1, waiting for transfers between devices, body(): shard_piece = lax.all_gather(logit_grad, 'exp', axis=0, tiled=True)  63.3 us
    psum x1, waiting for transfers between devices, body(): grad_router = lax.psum(weight_grad, 'tok')  57.3 us
    all_to_all x1, blocking collectives, body(): lax.all_to_all(sent_tokens, 'exp', split_axis=0, concat_axis=0, tiled=True)  28.4 us
  transfers between devices with their start and end apart: 9, of which 6 were waited for; matrix products, arithmetic and copies ran while one was open for 6% of the time, Pallas kernels for 0%

commit v1 on v0

v1 whole, which is shorter than its diff:
```python
import jax
import jax.numpy as jnp
from jax import lax
from jax.experimental import pallas as pl
from jax.experimental.pallas import tpu as pltpu
from jax.sharding import PartitionSpec as P

MESH = pl.DeviceIdType.MESH
BF = jnp.bfloat16
F32 = jnp.float32
NE = 64
NT = 8
CAP = 16
COLS = 4
NEAR = (0, 1, 7, 2, 6, 3, 5, 4)
FAR = (4, 3, 5, 2, 6, 1, 7, 0)
NN = (((1,), (0,)), ((), ()))
NTD = (((1,), (1,)), ((), ()))
TND = (((0,), (0,)), ((), ()))


def dot(a, b, dims):
    return lax.dot_general(a, b, dims, preferred_element_type=F32)


def remote(src, dst, send, recv, **where):
    return pltpu.make_async_remote_copy(
        src, dst, send, recv, device_id=where, device_id_type=MESH
    )


def kernel(
    tk, og, wr, plb, wg_h, wu_h, wd_h,
    out_layer, out_token, out_router,
    PT, S, R, G2, WS, WM, WRF, WG, WU, WD, ACC, ACT,
    PB, SB, PS, B1, B2, B3, C2, GPB, GPR, LQ, LQM, LQR, TS, TR, GRP, GRR, GRO, GRF, D3,
    wsem, loc, d_s, d_r, g_s, g_r, w1_s, w1_r, w2_s, w2_r, w3_s, w3_r,
    r_s, r_r, gg_s, gg_r, l1_s, l1_r, l2_s, l2_r, t_s, t_r, q1_s, q1_r, q2_s, q2_r,
):
    t = lax.axis_index("tok")
    me = lax.axis_index("exp")
    core = lax.rem(t, 2)
    x = t // 2
    y = me // 8
    z = lax.rem(me, 8)
    xr, xl, xo = lax.rem(x + 1, 4), lax.rem(x + 3, 4), lax.rem(x + 2, 4)
    sib = t + 1 - 2 * core
    right, left, opp = 2 * xr + core, 2 * xl + core, 2 * xo + core
    a = jnp.where(core == 0, y, z)
    b = jnp.where(core == 0, z, y)
    sa = jnp.where(core == 0, 8, 1)
    sb = jnp.where(core == 0, 1, 8)

    barrier = pltpu.get_barrier_semaphore()

    @pl.loop(1, NE)
    def _(k):
        pl.semaphore_signal(
            barrier, inc=1, device_id={"exp": lax.rem(me + k, NE)}, device_id_type=MESH
        )

    @pl.loop(1, NT)
    def _(k):
        pl.semaphore_signal(
            barrier, inc=1, device_id={"tok": lax.rem(t + k, NT)}, device_id_type=MESH
        )

    local = [
        pltpu.make_async_copy(wg_h, WG, wsem.at[0]),
        pltpu.make_async_copy(wu_h, WU, wsem.at[1]),
    ]
    for i in range(8):
        local.append(
            pltpu.make_async_copy(wd_h.at[:, pl.ds(512 * i, 512)], WD.at[i], wsem.at[2 + i])
        )
    for c in local:
        c.start()

    WS[...] = jnp.where(core == 0, wr[:, :128], wr[:, 128:])
    lane = lax.broadcasted_iota(jnp.int32, (128, 128), 1)

    @pl.loop(0, 8)
    def _(i):
        rows = pl.ds(pl.multiple_of(i * 128, 128), 128)
        pos = plb[rows, :]
        for c in range(16):
            PT[rows, c * 128 : (c + 1) * 128] = jnp.where(pos == lane + 128 * c, 1.0, 0.0).astype(BF)
        oh = PT[rows, :]
        got = jnp.concatenate((dot(oh, tk[...], NTD), dot(oh, og[...], NTD)), axis=1)
        S[pl.ds(i * 8, 8)] = got.astype(BF).reshape(8, 16, 128)

    pl.semaphore_wait(barrier, NE - 1 + NT - 1)

    for i, sh in enumerate(NEAR):
        row = lax.rem(y + sh, 8)

        @pl.loop(1 if sh == 0 else 0, 8)
        def _(k):
            d = row * 8 + lax.rem(z + k, 8)
            remote(S.at[d], R.at[me], d_s, d_r.at[i], exp=d).start()

        if sh == 0:
            pltpu.make_async_copy(S.at[me], R.at[me], d_r.at[0]).start()

    own_half = pltpu.make_async_copy(WS, WM.at[a], loc.at[0])
    own_half.start()
    w1 = []
    for k in range(1, 8):
        w1.append(remote(WS, WM.at[a], w1_s, w1_r, exp=lax.rem(a + k, 8) * sa + b * sb))
        w1[-1].start()

    def router_second():
        own_half.wait()
        seven = WM.at[pl.ds(0, 7)]
        remote(seven, seven, w1_s, w1_r, exp=me).wait_recv()
        cs = []
        for k in range(1, 8):
            cs.append(
                remote(WM, WRF.at[core, b], w2_s, w2_r.at[k], exp=a * sa + lax.rem(b + k, 8) * sb)
            )
            cs[-1].start()
        c = pltpu.make_async_copy(WM, WRF.at[core, b], loc.at[1])
        c.start()
        c.wait()
        cs.append(remote(WRF.at[core, b], WRF.at[core, b], w3_s.at[0], w3_r.at[0], tok=sib))
        cs[-1].start()
        return cs

    def router_third(k):
        src = lax.rem(b + 8 - k, 8)
        remote(WM, WRF.at[core, src], w2_s, w2_r.at[k], exp=me).wait_recv()
        c = remote(WRF.at[core, src], WRF.at[core, src], w3_s.at[k], w3_r.at[k], tok=sib)
        c.start()
        return c

    low = lax.broadcasted_iota(jnp.int32, (16, 128), 1) < 64
    sent = []
    kept = {}

    def go(key, c):
        c.start()
        sent.append(c)
        kept[key] = c

    def gather_own(i):
        row = lax.rem(y + 8 - NEAR[i], 8)
        eight = R.at[pl.ds(row * 8, 8)]
        remote(eight, eight, d_s, d_r.at[i], exp=me).wait_recv()
        for m in range(4):
            p = R[row * 8 + 2 * m].astype(F32)
            q = R[row * 8 + 2 * m + 1].astype(F32)
            cols = slice(128 * m, 128 * m + 128)
            G2[row, t, 0, :, cols] = jnp.where(low, p, pltpu.roll(q, 64, 1)).astype(BF)
            G2[row, t, 1, :, cols] = jnp.where(low, pltpu.roll(p, 64, 1), q).astype(BF)
        blk = G2.at[row, t]
        go((0, i), remote(blk, blk, g_s.at[0, i], g_r.at[0, i], tok=right))
        go((1, i), remote(blk, blk, g_s.at[1, i], g_r.at[1, i], tok=left))
        go((2, i), remote(blk, blk, g_s.at[2, i], g_r.at[2, i], tok=sib))

    def gather_next(i):
        row = lax.rem(y + 8 - NEAR[i], 8)
        blk = G2.at[row, left]
        remote(blk, blk, g_s.at[0, i], g_r.at[0, i], tok=right).wait_recv()
        part = G2.at[row, left, 0]
        go((3, i), remote(part, part, g_s.at[3, i], g_r.at[3, i], tok=right))
        go((4, i), remote(blk, blk, g_s.at[4, i], g_r.at[4, i], tok=sib))
        blk = G2.at[row, right]
        remote(blk, blk, g_s.at[1, i], g_r.at[1, i], tok=left).wait_recv()
        part = G2.at[row, right, 1]
        go((5, i), remote(part, part, g_s.at[5, i], g_r.at[5, i], tok=left))
        go((6, i), remote(blk, blk, g_s.at[6, i], g_r.at[6, i], tok=sib))

    def gather_far(i):
        row = lax.rem(y + 8 - NEAR[i], 8)
        for h, kind in ((0, 3), (1, 5)):
            part = G2.at[row, opp, h]
            remote(part, part, g_s.at[kind, i], g_r.at[kind, i], tok=right).wait_recv()
            go((7 + h, i), remote(part, part, g_s.at[7 + h, i], g_r.at[7 + h, i], tok=sib))

    def gather_done(i):
        row = lax.rem(y + 8 - NEAR[i], 8)
        side = 1 - core
        for kind, who in ((2, sib), (4, 2 * xl + side), (6, 2 * xr + side)):
            blk = G2.at[row, who]
            remote(blk, blk, g_s.at[kind, i], g_r.at[kind, i], tok=sib).wait_recv()
        for h in (0, 1):
            part = G2.at[row, 2 * xo + side, h]
            remote(part, part, g_s.at[7 + h, i], g_r.at[7 + h, i], tok=sib).wait_recv()
        rows = G2[row, :, 0].reshape(128, 512)
        grads = G2[row, :, 1].reshape(128, 512)
        k = pl.ds(pl.multiple_of(row * 512, 512), 512)
        parts = (dot(rows, WG[k, :], NN), dot(rows, WU[k, :], NN), dot(grads, WD[row], NTD))
        for n, part in enumerate(parts):
            ACC[n] = part if i == 0 else ACC[n] + part

    w2 = None
    w3 = []
    for s in range(11):
        if s < 8:
            gather_own(s)
        if s == 4:
            w2 = router_second()
        if 1 <= s < 9:
            gather_next(s - 1)
        if 2 <= s < 10:
            gather_far(s - 2)
        if s == 3:
            for c in local:
                c.wait()
        if 3 <= s:
            gather_done(s - 3)

    pre_gate, pre_up, back = ACC[0], ACC[1], ACC[2]
    sg = jax.nn.sigmoid(pre_gate)
    hidden = (pre_gate * sg * pre_up).astype(BF)
    ACT[0] = hidden
    ACT[1] = (back * pre_up * sg * (1.0 + pre_gate * (1.0 - sg))).astype(BF)
    ACT[2] = (back * pre_gate * sg).astype(BF)
    gsum = jnp.sum(hidden.astype(F32) * back, axis=1, keepdims=True)
    GPB[...] = jnp.broadcast_to(gsum, (128, 128)).reshape(8, 16, 128)
    for k in range(1, 8):
        d = lax.rem(t + k, 8)
        remote(GPB.at[d], GPR.at[t], gg_s, gg_r, tok=d).start()
    pltpu.make_async_copy(GPB.at[t], GPR.at[t], gg_r).start()

    def sum_make(i):
        row = lax.rem(y + FAR[i], 8)
        k = pl.ds(pl.multiple_of(row * 512, 512), 512)
        eo = dot(ACT[0], WD[row], NN)
        PB[i, 0] = eo.astype(BF).reshape(4, 2, 16, 512)
        ri = dot(ACT[1], WG[k, :], NTD) + dot(ACT[2], WU[k, :], NTD)
        PB[i, 1] = ri.astype(BF).reshape(4, 2, 16, 512)
        go(("sib", i), remote(PB.at[i, :, :, 1 - core], SB.at[i], r_s.at[0, i], r_r.at[0, i], tok=sib))

    def sum_pair(i):
        kept["sib", i].wait_recv()
        PS[i] = (PB[i, :, :, core].astype(F32) + SB[i].astype(F32)).astype(BF)
        go(("le", i), remote(PS.at[i, 0, xo], B1.at[i, 0], r_s.at[1, i], r_r.at[1, i], tok=right))
        go(("lr", i), remote(PS.at[i, 1, xo], B1.at[i, 1], r_s.at[2, i], r_r.at[2, i], tok=left))
        go(("de", i), remote(PS.at[i, 0, xl], B3.at[i, 0], r_s.at[3, i], r_r.at[3, i], tok=left))
        go(("dr", i), remote(PS.at[i, 1, xr], B3.at[i, 1], r_s.at[4, i], r_r.at[4, i], tok=right))

    def sum_next(i):
        kept["le", i].wait_recv()
        C2[i, 0] = (PS[i, 0, xr].astype(F32) + B1[i, 0].astype(F32)).astype(BF)
        go(("ce", i), remote(C2.at[i, 0], B2.at[i, 0], r_s.at[5, i], r_r.at[5, i], tok=right))
        kept["lr", i].wait_recv()
        C2[i, 1] = (PS[i, 1, xl].astype(F32) + B1[i, 1].astype(F32)).astype(BF)
        go(("cr", i), remote(C2.at[i, 1], B2.at[i, 1], r_s.at[6, i], r_r.at[6, i], tok=left))

    def router():
        logits = [jnp.zeros((16, 128), F32), jnp.zeros((16, 128), F32)]
        for r in range(8):
            own = G2[r, t, 0]
            logits[0] += dot(own, WRF[0, :, r].reshape(512, 128), NN)
            logits[1] += dot(own, WRF[1, r].reshape(512, 128), NN)
        peak = jnp.maximum(
            jnp.max(logits[0], axis=1, keepdims=True), jnp.max(logits[1], axis=1, keepdims=True)
        )
        ex = [jnp.exp(v - peak) for v in logits]
        total = jnp.sum(ex[0], axis=1, keepdims=True) + jnp.sum(ex[1], axis=1, keepdims=True)
        probs = [v / total for v in ex]
        at = lax.broadcasted_iota(jnp.int32, (16, 128), 1)
        hit = [at == me * COLS, at + 128 == me * COLS]
        weight = sum(
            jnp.sum(jnp.where(m, v, 0.0), axis=1, keepdims=True) for m, v in zip(hit, probs)
        )
        eight = GPR.at[pl.ds(0, 8)]
        remote(eight, eight, gg_s, gg_r, tok=t).wait_recv()
        gate = GPR[0]
        for k in range(1, 8):
            gate = gate + GPR[k]
        scale = gate * weight
        for n in range(2):
            diff = jnp.where(hit[n], 1.0, 0.0) - probs[n]
            LQ[:, 128 * n : 128 * n + 128] = (diff * scale).astype(BF)
            for p in range(3):
                piece = diff.astype(BF)
                D3[n, 16 * p : 16 * p + 16] = piece
                diff = diff - piece.astype(F32)
        own_lq = pltpu.make_async_copy(LQ, LQM.at[a], loc.at[2])
        own_lq.start()
        for k in range(1, 8):
            remote(LQ, LQM.at[a], l1_s, l1_r, exp=lax.rem(a + k, 8) * sa + b * sb).start()
        return weight, scale, own_lq

    def router_grad_second(own_lq):
        own_lq.wait()
        seven = LQM.at[pl.ds(0, 7)]
        remote(seven, seven, l1_s, l1_r, exp=me).wait_recv()
        for k in range(1, 8):
            remote(LQM, LQR.at[b], l2_s, l2_r, exp=a * sa + lax.rem(b + k, 8) * sb).start()
        own = pltpu.make_async_copy(LQM, LQR.at[b], loc.at[3])
        own.start()
        return own

    def router_grad_sum(own):
        own.wait()
        seven = LQR.at[pl.ds(0, 7)]
        remote(seven, seven, l2_s, l2_r, exp=me).wait_recv()
        total = jnp.zeros((128, 256), F32)
        Sv = S[...].reshape(8, 8, 16, 128)
        for n in range(8):
            rows = jnp.where(core == 0, Sv[:, n].astype(F32), Sv[n].astype(F32)).astype(BF)
            total = total + dot(rows.reshape(128, 128), LQR[n].reshape(128, 256), TND)
        GRP[...] = total[:64].reshape(8, 8, 256)
        for k in range(1, 8):
            d = lax.rem(t + k, 8)
            remote(GRP.at[d], GRR.at[t], q1_s, q1_r, tok=d).start()
        pltpu.make_async_copy(GRP.at[t], GRR.at[t], q1_r).start()

    def router_grad_share():
        eight = GRR.at[pl.ds(0, 8)]
        remote(eight, eight, q1_s, q1_r, tok=t).wait_recv()
        total = GRR[0]
        for k in range(1, 8):
            total = total + GRR[k]
        GRO[...] = total
        for k in range(1, 8):
            remote(GRO, GRF.at[t], q2_s, q2_r, tok=lax.rem(t + k, 8)).start()
        pltpu.make_async_copy(GRO, GRF.at[t], q2_r).start()

    def finish(i, weight, scale):
        row = lax.rem(y + FAR[i], 8)
        for key in ("de", "dr", "ce", "cr"):
            kept[key, i].wait_recv()
        eo = PS[i, 0, x].astype(F32) + B2[i, 0].astype(F32) + B3[i, 0].astype(F32)
        ri = PS[i, 1, x].astype(F32) + B2[i, 1].astype(F32) + B3[i, 1].astype(F32)
        v3 = dot(D3[0], WRF[0, :, row].reshape(512, 128), NTD)
        v3 = v3 + dot(D3[1], WRF[1, row].reshape(512, 128), NTD)
        v = v3[0:16] + v3[16:32] + v3[32:48]
        for m in range(4):
            cols = slice(128 * m, 128 * m + 128)
            w = eo[:, cols] * weight
            g = ri[:, cols] * weight + v[:, cols] * scale
            TS[row * 8 + 2 * m] = jnp.where(low, w, pltpu.roll(g, 64, 1)).astype(BF)
            TS[row * 8 + 2 * m + 1] = jnp.where(low, pltpu.roll(w, 64, 1), g).astype(BF)

        @pl.loop(1 if FAR[i] == 0 else 0, 8)
        def _(k):
            d = row * 8 + lax.rem(z + k, 8)
            remote(TS.at[d], TR.at[me], t_s, t_r, exp=d).start()

        if FAR[i] == 0:
            pltpu.make_async_copy(TS.at[me], TR.at[me], t_r).start()

    for s in range(3):
        sum_make(s)
        if s >= 1:
            sum_pair(s - 1)
        if s >= 2:
            sum_next(s - 2)
    for k in range(1, 8):
        w3.append(router_third(k))
    for k in range(8):
        src = lax.rem(jnp.where(core == 0, y, z) + 8 - k, 8)
        blk = WRF.at[1 - core, src]
        remote(blk, blk, w3_s.at[k], w3_r.at[k], tok=sib).wait_recv()
    weight, scale, own_lq = router()
    own = None
    for s in range(3, 11):
        if s < 8:
            sum_make(s)
        if s < 9:
            sum_pair(s - 1)
        if s < 10:
            sum_next(s - 2)
        finish(s - 3, weight, scale)
        if s == 5:
            own = router_grad_second(own_lq)
    router_grad_sum(own)
    router_grad_share()

    every = TR.at[pl.ds(0, 64)]
    remote(every, every, t_s, t_r, exp=me).wait_recv()
    back_rows = TR[...].reshape(1024, 128)

    for c in range(4):
        cols = slice(512 * c, 512 * c + 512)
        res = dot(back_rows, PT[:, cols], TND)
        out_layer[:, cols] = res[:64].astype(BF)
        out_token[:, cols] = res[64:].astype(BF)

    eight = GRF.at[pl.ds(0, 8)]
    remote(eight, eight, q2_s, q2_r, tok=t).wait_recv()
    out_router[...] = GRF[...].reshape(64, 256)

    for c in sent + w3 + w2[7:]:
        c.wait_send()
    n63 = S.at[pl.ds(0, 63)]
    remote(n63, n63, d_s, d_r.at[0], exp=me).wait_send()
    remote(n63, n63, t_s, t_r, exp=me).wait_send()
    n7 = WM.at[pl.ds(0, 7)]
    remote(n7, n7, w1_s, w1_r, exp=me).wait_send()
    n7 = WRF.at[0, pl.ds(0, 7)]
    remote(n7, n7, w2_s, w2_r.at[1], exp=me).wait_send()
    n7 = GPB.at[pl.ds(0, 7)]
    remote(n7, n7, gg_s, gg_r, tok=t).wait_send()
    n7 = LQM.at[pl.ds(0, 7)]
    remote(n7, n7, l1_s, l1_r, exp=me).wait_send()
    n7 = LQR.at[pl.ds(0, 7)]
    remote(n7, n7, l2_s, l2_r, exp=me).wait_send()
    n7 = GRP.at[pl.ds(0, 7)]
    remote(n7, n7, q1_s, q1_r, tok=t).wait_send()
    remote(n7, n7, q2_s, q2_r, tok=t).wait_send()


def body(tokens, w_router, pick_lists, w_gate, w_up, w_down, out_grad):
    flat = jnp.broadcast_to(pick_lists.reshape(NE * CAP, 1), (NE * CAP, 128))
    V = pltpu.VMEM
    D = pltpu.SemaphoreType.DMA
    vm = pl.BlockSpec(memory_space=pltpu.VMEM)
    hbm = pl.BlockSpec(memory_space=pl.ANY)
    scratch = [
        V((1024, 2048), BF),
        V((64, 16, 128), BF),
        V((64, 16, 128), BF),
        V((8, 8, 2, 16, 512), BF),
        V((64, 128), BF),
        V((8, 64, 128), BF),
        V((2, 8, 8, 64, 128), BF),
        V((4096, 128), BF),
        V((4096, 128), BF),
        V((8, 128, 512), BF),
        V((3, 128, 128), F32),
        V((3, 128, 128), BF),
        V((8, 2, 4, 2, 16, 512), BF),
        V((8, 2, 4, 16, 512), BF),
        V((8, 2, 4, 16, 512), BF),
        V((8, 2, 16, 512), BF),
        V((8, 2, 16, 512), BF),
        V((8, 2, 16, 512), BF),
        V((8, 2, 16, 512), BF),
        V((8, 16, 128), F32),
        V((8, 16, 128), F32),
        V((16, 256), BF),
        V((8, 16, 256), BF),
        V((8, 8, 16, 256), BF),
        V((64, 16, 128), BF),
        V((64, 16, 128), BF),
        V((8, 8, 256), F32),
        V((8, 8, 256), F32),
        V((8, 256), F32),
        V((8, 8, 256), F32),
        V((2, 48, 128), BF),
        D((10,)), D((4,)),
        D, D((8,)),
        D((9, 8)), D((9, 8)),
        D, D,
        D, D((8,)),
        D((8,)), D((8,)),
        D((7, 8)), D((7, 8)),
        D, D,
        D, D, D, D,
        D, D,
        D, D, D, D,
    ]
    return pl.pallas_call(
        kernel,
        out_shape=(
            jax.ShapeDtypeStruct((64, 2048), BF),
            jax.ShapeDtypeStruct((64, 2048), BF),
            jax.ShapeDtypeStruct((64, 256), F32),
        ),
        in_specs=[vm, vm, vm, vm, hbm, hbm, hbm],
        out_specs=(vm, vm, vm),
        scratch_shapes=scratch,
        compiler_params=pltpu.CompilerParams(
            collective_id=0, has_side_effects=True, vmem_limit_bytes=48 << 20
        ),
        cost_estimate=pl.CostEstimate(
            flops=3_000_000_000, bytes_accessed=8_000_000, transcendentals=40_000
        ),
        name="experts",
    )(tokens, out_grad, w_router, flat, w_gate[0], w_up[0], w_down[0])


def solution(mesh):
    placed = (
        P("exp", "tok"),
        P("exp", None),
        P("tok", None, None),
        P("exp", None, "tok"),
        P("exp", None, "tok"),
        P("exp", "tok", None),
        P("exp", "tok"),
    )
    return jax.shard_map(
        body,
        mesh=mesh,
        in_specs=placed,
        out_specs=(P("exp", "tok"), P("exp", "tok"), P("exp", None)),
        check_vma=False,
    )
```

time: 828 us -> 94.9 us (0.11)
  blocking collectives: 391 us -> 0 us
  waiting for transfers between devices: 331 us -> 0 us
  Pallas kernels: 0 us -> 86.4 us
  other arithmetic: 25.9 us -> 0 us
  local copies, waits for them, and re-layouts: 31.2 us -> 7.59 us
  starting transfers between devices: 17.7 us -> 0 us
  between operations: 16.4 us -> 0.66 us
  matrix products: 13.2 us -> 0 us
    psum x2 -> x0, blocking collectives: 231 us -> none  [the longest x1 119 us: body(): pick_sum = lax.psum(router_probs[0] * own_score_grad, 'exp')]
    all_gather x3 -> x0, waiting for transfers between devices: 168 us -> none  [the longest x1 84.7 us: body(): lax.all_gather(row_grad, 'tok', axis=1, tiled=True)]
    pmax x1 -> x0, blocking collectives: 115 us -> none  [body(): peak_score = lax.pmax(jnp.max(local_logits, axis=0), 'exp')]
    unnamed x8 -> x0, waiting for transfers between devices: 95.6 us -> none
    pallas_call x0 -> x1, Pallas kernels: none -> 86.4 us  [body(): pl.pallas_call(kernel, out_shape=(jax.ShapeDtypeStruct((64, 2048), BF), j...]
    psum x1 -> x0, waiting for transfers between devices: 57.3 us -> none  [body(): grad_router = lax.psum(weight_grad, 'tok')]
    all_to_all x2 -> x0, blocking collectives: 44.9 us -> none  [the longest x1 28.4 us: body(): lax.all_to_all(sent_tokens, 'exp', split_axis=0, concat_axis=0, tiled=True)]
    all_to_all x2 -> x0, starting transfers between devices: 17.5 us -> none  [the longest x1 12.8 us: body(): lax.all_to_all(sent_grads, 'exp', split_axis=0, concat_axis=0, tiled=True)]
  transfers between devices with their start and end apart: 9 -> 0, of which waited for: 6 -> 0; matrix products, arithmetic and copies ran while one was open for 6% -> 0% of each run, Pallas kernels for 0% -> 0%
where the time goes in v1:
time: 94.9 us; the launch traced here: 94.6 us
  Pallas kernels  86.4 us (91%)
  local copies, waits for them, and re-layouts  7.59 us (8%)
    pallas_call x1, Pallas kernels, body(): pl.pallas_call(kernel, out_shape=(jax.ShapeDtypeStruct((64, 2048), BF), j...  86.4 us
    unnamed x16, local copies, waits for them, and re-layouts  7.32 us

profile of v1, /device:TPU:1, one launch (start us, length us, event | category | flops | bytes accessed | tf_op | source)
XLA Modules:
  0.0 94.6 jit_solution(11487049989434579319)
XLA Ops:
  0.6 0.8 copy.10
  1.4 0.0 copy-start.5
  1.4 0.1 broadcast_in_dim.7
  1.5 0.0 copy-start.3
  1.5 0.0 copy-start.4
  1.5 0.2 broadcast_in_dim.8.plb
  1.7 0.5 copy-done.5
  2.2 0.3 copy-done.3
  2.4 0.1 copy-done.4
  2.5 0.0 copy-start
  2.5 1.2 %copy-done = bf16[1,4096,128]{2,1,0:T(8,128)(2,1)S(1)} copy-done((bf16[1,4096,128]{2,1,0:T(8,128)(2,1)S(1)}, bf16[1,4096,128]{2,1,0:T(8,128)(2,1)}, u32[]{:S(2)}) %copy-start) | copy-done | bytes 1048600
  3.7 0.0 copy-start.1
  3.8 1.2 %copy-done.1 = bf16[1,4096,128]{2,1,0:T(8,128)(2,1)S(1)} copy-done((bf16[1,4096,128]{2,1,0:T(8,128)(2,1)S(1)}, bf16[1,4096,128]{2,1,0:T(8,128)(2,1)}, u32[]{:S(2)}) %copy-start.1) | copy-done | bytes 1048600
  5.0 0.0 copy-start.2
  5.0 1.2 %copy-done.2 = bf16[1,128,4096]{2,1,0:T(8,128)(2,1)S(1)} copy-done((bf16[1,128,4096]{2,1,0:T(8,128)(2,1)S(1)}, bf16[1,128,4096]{2,1,0:T(8,128)(2,1)}, u32[]{:S(2)}) %copy-start.2) | copy-done | bytes 1048600
  6.2 86.4 %experts.1 = (bf16[64,2048]{1,0:T(8,128)(2,1)S(1)}, bf16[64,2048]{1,0:T(8,128)(2,1)S(1)}, f32[64,256]{1,0:T(8,128)S(1)}) custom-call(bf16[64,2048]{1,0:T(8,128)(2,1)S(1)} %copy-done.3, bf16[64,2048]{1,0:T(8,128)(2,1)S(1)} %copy-done.4, bf16[64,256]{1,0:T(8,128)(2,1)S(1)} %copy-done.5, s32[1024,128]{1,0:T(8,128)S(1)} %broadcast_in_dim.8.plb, ...), custom_call_target="tpu_custom_call" | custom-call | flops 3000000000 | bytes 8000000 | tf_op jit(solution)/shard_map/experts/pallas_call | solution.py:458
  92.6 0.7 copy.14
  93.3 0.7 copy.15
  94.0 0.6 copy.16
Async XLA Ops:
  1.4 0.8 copy-start.5
  1.5 1.0 %copy-start.3 = (bf16[64,2048]{1,0:T(8,128)(2,1)S(1)}, bf16[64,2048]{1,0:T(8,128)(2,1)}, u32[]{:S(2)}) copy-start(bf16[64,2048]{1,0:T(8,128)(2,1)} %tk.1) | copy-start | bytes 786436
  1.5 1.0 %copy-start.4 = (bf16[64,2048]{1,0:T(8,128)(2,1)S(1)}, bf16[64,2048]{1,0:T(8,128)(2,1)}, u32[]{:S(2)}) copy-start(bf16[64,2048]{1,0:T(8,128)(2,1)} %og.1) | copy-start | bytes 786436
  2.5 1.2 %copy-start = (bf16[1,4096,128]{2,1,0:T(8,128)(2,1)S(1)}, bf16[1,4096,128]{2,1,0:T(8,128)(2,1)}, u32[]{:S(2)}) copy-start(bf16[1,4096,128]{2,1,0:T(8,128)(2,1)} %param.10) | copy-start | bytes 3145732
  3.7 1.2 %copy-start.1 = (bf16[1,4096,128]{2,1,0:T(8,128)(2,1)S(1)}, bf16[1,4096,128]{2,1,0:T(8,128)(2,1)}, u32[]{:S(2)}) copy-start(bf16[1,4096,128]{2,1,0:T(8,128)(2,1)} %param.11) | copy-start | bytes 3145732
  5.0 1.2 %copy-start.2 = (bf16[1,128,4096]{2,1,0:T(8,128)(2,1)S(1)}, bf16[1,128,4096]{2,1,0:T(8,128)(2,1)}, u32[]{:S(2)}) copy-start(bf16[1,128,4096]{2,1,0:T(8,128)(2,1)} %param.12) | copy-start | bytes 3145732

commit v2 on v1

--- a/solution.py
+++ b/solution.py
@@ -14,6 +14,12 @@
 COLS = 4
 NEAR = (0, 1, 7, 2, 6, 3, 5, 4)
 FAR = (4, 3, 5, 2, 6, 1, 7, 0)
+AHEAD = 8
+LAG = (3, 6, 8)
+SLAG = (2, 4, 6)
+RELAY = 8
+ROUTE = (3, 6, 10, 13)
+BACK = 3
 NN = (((1,), (0,)), ((), ()))
 NTD = (((1,), (1,)), ((), ()))
 TND = (((0,), (0,)), ((), ()))
@@ -30,10 +36,10 @@
 
 
 def kernel(
-    tk, og, wr, plb, wg_h, wu_h, wd_h,
+    tk_h, og_h, wr_h, pl_h, wg_h, wu_h, wd_h,
     out_layer, out_token, out_router,
-    PT, S, R, G2, WS, WM, WRF, WG, WU, WD, ACC, ACT,
-    PB, SB, PS, B1, B2, B3, C2, GPB, GPR, LQ, LQM, LQR, TS, TR, GRP, GRR, GRO, GRF, D3,
+    TK, OG, WRL, PLV, PT, S, R, G2, WS, WM, WRF, WG, WU, WD, ACC, ACT,
+    PB, SB, PS, B1, B2, B3, C2, GPB, GPR, LQ, LQM, LQR, TS, TR, GRP, GRR, GRO, GRF, D3, OUT,
     wsem, loc, d_s, d_r, g_s, g_r, w1_s, w1_r, w2_s, w2_r, w3_s, w3_r,
     r_s, r_r, gg_s, gg_r, l1_s, l1_r, l2_s, l2_r, t_s, t_r, q1_s, q1_r, q2_s, q2_r,
 ):
@@ -53,6 +59,15 @@
 
     barrier = pltpu.get_barrier_semaphore()
 
+    first = [
+        pltpu.make_async_copy(pl_h, PLV, loc.at[4]),
+        pltpu.make_async_copy(tk_h, TK, loc.at[5]),
+        pltpu.make_async_copy(og_h, OG, loc.at[6]),
+        pltpu.make_async_copy(wr_h, WRL, loc.at[7]),
+    ]
+    for c in first:
+        c.start()
+
     @pl.loop(1, NE)
     def _(k):
         pl.semaphore_signal(
@@ -76,23 +91,32 @@
     for c in local:
         c.start()
 
-    WS[...] = jnp.where(core == 0, wr[:, :128], wr[:, 128:])
     lane = lax.broadcasted_iota(jnp.int32, (128, 128), 1)
-
-    @pl.loop(0, 8)
-    def _(i):
-        rows = pl.ds(pl.multiple_of(i * 128, 128), 128)
-        pos = plb[rows, :]
+    expert = lax.broadcasted_iota(jnp.int32, (16, 64), 1)
+
+    def pick_row(row):
+        cols = []
+        for n in range(8):
+            line = jnp.where(expert == row * 8 + n, PLV[...].astype(F32), 0.0)
+            cols.append(jnp.sum(line, axis=1, keepdims=True))
+        pos = jnp.broadcast_to(jnp.concatenate(cols, axis=0).astype(jnp.int32), (128, 128))
+        rows = pl.ds(pl.multiple_of(row * 128, 128), 128)
         for c in range(16):
             PT[rows, c * 128 : (c + 1) * 128] = jnp.where(pos == lane + 128 * c, 1.0, 0.0).astype(BF)
         oh = PT[rows, :]
-        got = jnp.concatenate((dot(oh, tk[...], NTD), dot(oh, og[...], NTD)), axis=1)
-        S[pl.ds(i * 8, 8)] = got.astype(BF).reshape(8, 16, 128)
-
-    pl.semaphore_wait(barrier, NE - 1 + NT - 1)
-
-    for i, sh in enumerate(NEAR):
+        got = jnp.concatenate((dot(oh, TK[...], NTD), dot(oh, OG[...], NTD)), axis=1)
+        S[pl.ds(row * 8, 8)] = got.astype(BF).reshape(8, 16, 128)
+
+    for c in first:
+        c.wait()
+    WS[...] = jnp.where(core == 0, WRL[:, :128], WRL[:, 128:])
+
+    def dispatch(i):
+        sh = NEAR[i]
         row = lax.rem(y + sh, 8)
+        pick_row(row)
+        if i == 0:
+            pl.semaphore_wait(barrier, NE - 1 + NT - 1)
 
         @pl.loop(1 if sh == 0 else 0, 8)
         def _(k):
@@ -101,6 +125,9 @@
 
         if sh == 0:
             pltpu.make_async_copy(S.at[me], R.at[me], d_r.at[0]).start()
+
+    for i in range(AHEAD):
+        dispatch(i)
 
     own_half = pltpu.make_async_copy(WS, WM.at[a], loc.at[0])
     own_half.start()
@@ -195,20 +222,24 @@
 
     w2 = None
     w3 = []
-    for s in range(11):
+    for s in range(8 + LAG[2]):
+        if s + AHEAD < 8:
+            dispatch(s + AHEAD)
         if s < 8:
             gather_own(s)
         if s == 4:
             w2 = router_second()
-        if 1 <= s < 9:
-            gather_next(s - 1)
-        if 2 <= s < 10:
-            gather_far(s - 2)
-        if s == 3:
+        if 0 <= s - LAG[0] < 8:
+            gather_next(s - LAG[0])
+        if 0 <= s - LAG[1] < 8:
+            gather_far(s - LAG[1])
+        if s == LAG[2]:
             for c in local:
                 c.wait()
-        if 3 <= s:
-            gather_done(s - 3)
+        if 0 <= s - LAG[2] < 8:
+            gather_done(s - LAG[2])
+        if 1 <= s - RELAY < 8:
+            w3.append(router_third(s - RELAY))
 
     pre_gate, pre_up, back = ACC[0], ACC[1], ACC[2]
     sg = jax.nn.sigmoid(pre_gate)
@@ -339,47 +370,62 @@
         @pl.loop(1 if FAR[i] == 0 else 0, 8)
         def _(k):
             d = row * 8 + lax.rem(z + k, 8)
-            remote(TS.at[d], TR.at[me], t_s, t_r, exp=d).start()
+            remote(TS.at[d], TR.at[me], t_s, t_r.at[i], exp=d).start()
 
         if FAR[i] == 0:
-            pltpu.make_async_copy(TS.at[me], TR.at[me], t_r).start()
-
-    for s in range(3):
-        sum_make(s)
-        if s >= 1:
-            sum_pair(s - 1)
-        if s >= 2:
-            sum_next(s - 2)
-    for k in range(1, 8):
-        w3.append(router_third(k))
-    for k in range(8):
-        src = lax.rem(jnp.where(core == 0, y, z) + 8 - k, 8)
-        blk = WRF.at[1 - core, src]
-        remote(blk, blk, w3_s.at[k], w3_r.at[k], tok=sib).wait_recv()
-    weight, scale, own_lq = router()
-    own = None
-    for s in range(3, 11):
+            pltpu.make_async_copy(TS.at[me], TR.at[me], t_r.at[i]).start()
+
+    def router_ready():
+        for k in range(8):
+            src = lax.rem(jnp.where(core == 0, y, z) + 8 - k, 8)
+            blk = WRF.at[1 - core, src]
+            remote(blk, blk, w3_s.at[k], w3_r.at[k], tok=sib).wait_recv()
+
+    def add_back(blocks, first, last):
+        rows = []
+        for i in blocks:
+            rows.append(lax.rem(y + 8 - FAR[i], 8))
+            eight = TR.at[pl.ds(rows[-1] * 8, 8)]
+            remote(eight, eight, t_s, t_r.at[i], exp=me).wait_recv()
+        tiles = [TR[pl.ds(r * 8, 8)].reshape(128, 128) for r in rows]
+        for c in range(4):
+            cols = slice(512 * c, 512 * c + 512)
+            res = None if first else OUT[:, cols]
+            for r, tile in zip(rows, tiles):
+                hot = PT[pl.ds(pl.multiple_of(r * 128, 128), 128), cols]
+                part = dot(tile, hot, TND)
+                res = part if res is None else res + part
+            if last:
+                out_layer[:, cols] = res[:64].astype(BF)
+                out_token[:, cols] = res[64:].astype(BF)
+            else:
+                OUT[:, cols] = res
+
+    for s in range(8 + SLAG[2] + BACK):
         if s < 8:
             sum_make(s)
-        if s < 9:
-            sum_pair(s - 1)
-        if s < 10:
-            sum_next(s - 2)
-        finish(s - 3, weight, scale)
-        if s == 5:
+        if 0 <= s - SLAG[0] < 8:
+            sum_pair(s - SLAG[0])
+        if 0 <= s - SLAG[1] < 8:
+            sum_next(s - SLAG[1])
+        if s == ROUTE[0]:
+            router_ready()
+            weight, scale, own_lq = router()
+        if s == ROUTE[1]:
             own = router_grad_second(own_lq)
-    router_grad_sum(own)
-    router_grad_share()
-
-    every = TR.at[pl.ds(0, 64)]
-    remote(every, every, t_s, t_r, exp=me).wait_recv()
-    back_rows = TR[...].reshape(1024, 128)
-
-    for c in range(4):
-        cols = slice(512 * c, 512 * c + 512)
-        res = dot(back_rows, PT[:, cols], TND)
-        out_layer[:, cols] = res[:64].astype(BF)
-        out_token[:, cols] = res[64:].astype(BF)
+        if s == ROUTE[2]:
+            router_grad_sum(own)
+        if s == ROUTE[3]:
+            router_grad_share()
+        if 0 <= s - SLAG[2] < 8:
+            finish(s - SLAG[2], weight, scale)
+        done = s - SLAG[2] - BACK
+        if done == 3:
+            add_back(range(0, 4), True, False)
+        if done == 6:
+            add_back(range(4, 7), False, False)
+        if done == 7:
+            add_back(range(7, 8), False, True)
 
     eight = GRF.at[pl.ds(0, 8)]
     remote(eight, eight, q2_s, q2_r, tok=t).wait_recv()
@@ -389,7 +435,7 @@
         c.wait_send()
     n63 = S.at[pl.ds(0, 63)]
     remote(n63, n63, d_s, d_r.at[0], exp=me).wait_send()
-    remote(n63, n63, t_s, t_r, exp=me).wait_send()
+    remote(n63, n63, t_s, t_r.at[0], exp=me).wait_send()
     n7 = WM.at[pl.ds(0, 7)]
     remote(n7, n7, w1_s, w1_r, exp=me).wait_send()
     n7 = WRF.at[0, pl.ds(0, 7)]
@@ -406,12 +452,15 @@
 
 
 def body(tokens, w_router, pick_lists, w_gate, w_up, w_down, out_grad):
-    flat = jnp.broadcast_to(pick_lists.reshape(NE * CAP, 1), (NE * CAP, 128))
     V = pltpu.VMEM
     D = pltpu.SemaphoreType.DMA
     vm = pl.BlockSpec(memory_space=pltpu.VMEM)
     hbm = pl.BlockSpec(memory_space=pl.ANY)
     scratch = [
+        V((64, 2048), BF),
+        V((64, 2048), BF),
+        V((64, 256), BF),
+        V((16, 64), jnp.int32),
         V((1024, 2048), BF),
         V((64, 16, 128), BF),
         V((64, 16, 128), BF),
@@ -443,7 +492,8 @@
         V((8, 256), F32),
         V((8, 8, 256), F32),
         V((2, 48, 128), BF),
-        D((10,)), D((4,)),
+        V((128, 2048), F32),
+        D((10,)), D((8,)),
         D, D((8,)),
         D((9, 8)), D((9, 8)),
         D, D,
@@ -452,27 +502,47 @@
         D((7, 8)), D((7, 8)),
         D, D,
         D, D, D, D,
-        D, D,
+        D, D((8,)),
         D, D, D, D,
     ]
-    return pl.pallas_call(
+    shapes = (
+        jax.ShapeDtypeStruct((64, 2048), BF),
+        jax.ShapeDtypeStruct((64, 2048), BF),
+        jax.ShapeDtypeStruct((64, 256), F32),
+    )
+    results = pl.pallas_call(
         kernel,
-        out_shape=(
-            jax.ShapeDtypeStruct((64, 2048), BF),
-            jax.ShapeDtypeStruct((64, 2048), BF),
-            jax.ShapeDtypeStruct((64, 256), F32),
-        ),
-        in_specs=[vm, vm, vm, vm, hbm, hbm, hbm],
+        out_shape=shapes,
+        in_specs=[hbm] * 7,
         out_specs=(vm, vm, vm),
         scratch_shapes=scratch,
         compiler_params=pltpu.CompilerParams(
-            collective_id=0, has_side_effects=True, vmem_limit_bytes=48 << 20
+            collective_id=0, has_side_effects=True, vmem_limit_bytes=60 << 20
         ),
         cost_estimate=pl.CostEstimate(
             flops=3_000_000_000, bytes_accessed=8_000_000, transcendentals=40_000
         ),
         name="experts",
-    )(tokens, out_grad, w_router, flat, w_gate[0], w_up[0], w_down[0])
+    )(tokens, out_grad, w_router, pick_lists[0].T, w_gate[0], w_up[0], w_down[0])
+    return pl.pallas_call(
+        hand_over,
+        out_shape=shapes,
+        in_specs=[vm] * 3,
+        out_specs=(hbm,) * 3,
+        scratch_shapes=[D((3,))],
+        name="results",
+    )(*results)
+
+
+def hand_over(a, b, c, ra, rb, rc, sem):
+    copies = [
+        pltpu.make_async_copy(src, dst, sem.at[n])
+        for n, (src, dst) in enumerate(((a, ra), (b, rb), (c, rc)))
+    ]
+    for copy in copies:
+        copy.start()
+    for copy in copies:
+        copy.wait()
 
 
 def solution(mesh):

time: 94.9 us -> 81.3 us (0.86)
  local copies, waits for them, and re-layouts: 7.59 us -> 0 us
  Pallas kernels: 86.4 us -> 80.5 us
    unnamed x16 -> x0, local copies, waits for them, and re-layouts: 7.32 us -> none
    pallas_call x1 -> x2, Pallas kernels: 86.4 us -> 80.5 us  [the longest x1 78.7 us: body(): pl.pallas_call(kernel, out_shape=shapes, in_specs=[hbm] * 7, out_specs=(v...]
where the time goes in v2:
time: 81.3 us; the launch traced here: 81.2 us
  Pallas kernels  80.5 us (99%)
    pallas_call x1, Pallas kernels, body(): pl.pallas_call(kernel, out_shape=shapes, in_specs=[hbm] * 7, out_specs=(v...  78.7 us
    pallas_call x1, Pallas kernels, body(): pl.pallas_call(hand_over, out_shape=shapes, in_specs=[vm] * 3, out_specs=...  1.86 us

profile of v2, /device:TPU:1, one launch (start us, length us, event | category | flops | bytes accessed | tf_op | source)
XLA Modules:
  0.0 81.2 jit_solution(18406973675808807938)
XLA Ops:
  0.6 78.7 %experts.1 = (bf16[64,2048]{1,0:T(8,128)(2,1)}, bf16[64,2048]{1,0:T(8,128)(2,1)}, f32[64,256]{1,0:T(8,128)}) custom-call(bf16[64,2048]{1,0:T(8,128)(2,1)} %tk_h.1, bf16[64,2048]{1,0:T(8,128)(2,1)} %og_h.1, bf16[64,256]{1,0:T(8,128)(2,1)} %wr_h.1, s32[16,64]{1,0:T(8,128)} %bitcast.9, bf16[4096,128]{1,0:T(8,128)(2,1)} %bitcast.6, bf16[4096,128]{1,0:T(8,128)(2,1)} %bitcast.7, ...), custom_call_target="tpu_custom_call" | custom-call | flops 3000000000 | bytes 8000000 | tf_op jit(solution)/shard_map/experts/pallas_call | solution.py:513
  79.3 1.9 %results.1 = (bf16[64,2048]{1,0:T(8,128)(2,1)}, bf16[64,2048]{1,0:T(8,128)(2,1)}, f32[64,256]{1,0:T(8,128)}) custom-call(bf16[64,2048]{1,0:T(8,128)(2,1)} %get-tuple-element.6.a, bf16[64,2048]{1,0:T(8,128)(2,1)} %get-tuple-element.7.b, f32[64,256]{1,0:T(8,128)} %get-tuple-element.8.c), custom_call_target="tpu_custom_call" | custom-call | tf_op jit(solution)/shard_map/results/pallas_call | solution.py:527

commit v3 on v2

--- a/solution.py
+++ b/solution.py
@@ -18,7 +18,7 @@
 LAG = (3, 6, 8)
 SLAG = (2, 4, 6)
 RELAY = 8
-ROUTE = (3, 6, 10, 13)
+ROUTE = (2, 5, 9, 12)
 BACK = 3
 NN = (((1,), (0,)), ((), ()))
 NTD = (((1,), (1,)), ((), ()))
@@ -68,14 +68,12 @@
     for c in first:
         c.start()
 
-    @pl.loop(1, NE)
-    def _(k):
+    for k in range(1, NE):
         pl.semaphore_signal(
             barrier, inc=1, device_id={"exp": lax.rem(me + k, NE)}, device_id_type=MESH
         )
 
-    @pl.loop(1, NT)
-    def _(k):
+    for k in range(1, NT):
         pl.semaphore_signal(
             barrier, inc=1, device_id={"tok": lax.rem(t + k, NT)}, device_id_type=MESH
         )

time: 81.3 us -> 84.1 us (1.034)
  Pallas kernels: 80.5 us -> 83.3 us
    pallas_call x1, Pallas kernels: 78.7 us -> 81.5 us  [body(): pl.pallas_call(kernel, out_shape=shapes, in_specs=[hbm] * 7, out_specs=(v...]
where the time goes in v3:
time: 84.1 us; the launch traced here: 84 us
  Pallas kernels  83.3 us (99%)
    pallas_call x1, Pallas kernels, body(): pl.pallas_call(kernel, out_shape=shapes, in_specs=[hbm] * 7, out_specs=(v...  81.5 us
    pallas_call x1, Pallas kernels, body(): pl.pallas_call(hand_over, out_shape=shapes, in_specs=[vm] * 3, out_specs=...  1.86 us

profile of v3, /device:TPU:1, one launch (start us, length us, event | category | flops | bytes accessed | tf_op | source)
XLA Modules:
  0.0 84.0 jit_solution(9259450946474436391)
XLA Ops:
  0.6 81.5 %experts.1 = (bf16[64,2048]{1,0:T(8,128)(2,1)}, bf16[64,2048]{1,0:T(8,128)(2,1)}, f32[64,256]{1,0:T(8,128)}) custom-call(bf16[64,2048]{1,0:T(8,128)(2,1)} %tk_h.1, bf16[64,2048]{1,0:T(8,128)(2,1)} %og_h.1, bf16[64,256]{1,0:T(8,128)(2,1)} %wr_h.1, s32[16,64]{1,0:T(8,128)} %bitcast.9, bf16[4096,128]{1,0:T(8,128)(2,1)} %bitcast.6, bf16[4096,128]{1,0:T(8,128)(2,1)} %bitcast.7, ...), custom_call_target="tpu_custom_call" | custom-call | flops 3000000000 | bytes 8000000 | tf_op jit(solution)/shard_map/experts/pallas_call | solution.py:511
  82.1 1.9 %results.1 = (bf16[64,2048]{1,0:T(8,128)(2,1)}, bf16[64,2048]{1,0:T(8,128)(2,1)}, f32[64,256]{1,0:T(8,128)}) custom-call(bf16[64,2048]{1,0:T(8,128)(2,1)} %get-tuple-element.6.a, bf16[64,2048]{1,0:T(8,128)(2,1)} %get-tuple-element.7.b, f32[64,256]{1,0:T(8,128)} %get-tuple-element.8.c), custom_call_target="tpu_custom_call" | custom-call | tf_op jit(solution)/shard_map/results/pallas_call | solution.py:525
